TPU v7x, 32 devices: a whole 2x2x4 slice. The times are simulated.
32 devices in a mesh: dp: 8 (over z, y), tensor: 4 (over x, core).
Axes of the slice: x: 2, y: 2, z: 4, core: 2. Of those that a mesh axis runs over, the one named last changes fastest.
Arguments:
- layer_input: bfloat16 [10240, 768], P(('dp', 'tensor')), may hold values from -6 to 6
- cotangent: bfloat16 [10240, 768], P(('dp', 'tensor')), may hold values from -6 to 6
- segments: int32 [10240], replicated, may hold values from 0 to 25, as said below
- parents: int32 [26], replicated, may hold values from 0 to 17, as said below
- norm1_gain: bfloat16 [768], P('dp'), may hold values from 0.099609375 to 1.8984375
- w_query: bfloat16 [768, 768], P('dp', 'tensor'), may hold values from -0.21875 to 0.21875
- w_key: bfloat16 [768, 768], P('dp', 'tensor'), may hold values from -0.21875 to 0.21875
- w_value: bfloat16 [768, 768], P('dp', 'tensor'), may hold values from -0.21875 to 0.21875
- w_out: bfloat16 [768, 768], P('tensor', 'dp'), may hold values from -1.75 to 1.75
- norm2_gain: bfloat16 [768], P('dp'), may hold values from 0.099609375 to 1.8984375
- w_up: bfloat16 [768, 3072], P('dp', 'tensor'), may hold values from -0.21875 to 0.21875
- w_down: bfloat16 [3072, 768], P('tensor', 'dp'), may hold values from -0.109375 to 0.109375
Outputs:
- layer_output: bfloat16 [10240, 768], P(('dp', 'tensor'))
- input_grad: bfloat16 [10240, 768], P(('dp', 'tensor'))
- grad_norm1_gain: float32 [768], P('dp')
- grad_query: float32 [768, 768], P('dp', 'tensor')
- grad_key: float32 [768, 768], P('dp', 'tensor')
- grad_value: float32 [768, 768], P('dp', 'tensor')
- grad_out: float32 [768, 768], P('tensor', 'dp')
- grad_norm2_gain: float32 [768], P('dp')
- grad_up: float32 [768, 3072], P('dp', 'tensor')
- grad_down: float32 [3072, 768], P('tensor', 'dp')
Inputs may be any that keep to these rules, and one draw needn't show every extreme that they name: Tree t holds bytes 5120 t to 5120 (t + 1) - 1 of the stream (the last tree may end at 10240). Its first 2048 bytes are segment 13 t, the trunk; the rest are twelve runs of 256 bytes with the segments 13 t + 1 to 13 t + 12 in some order, every run after the run of its parent segment. parents[s] is the parent segment of s: the trunk 13 t is its own parent, the branches 13 t + 1 to 13 t + 4 have the trunk, and the leaves 13 t + 5 to 13 t + 12 have one of the four branches each, two leaves a branch.
All inputs are finite; a program needn't handle non-finite values.
Results may differ from a plain program's by a relative error of at most 0.017.
Values may be sent and summed in bfloat16 or wider, within the bound.
A program may use at most 256 MiB of HBM per device.

v0:
```python
import math
import jax
import jax.numpy as jnp
from jax import lax
from jax.sharding import PartitionSpec as P

HD = 64
WINDOW = 1536
epsilon = 1e-06
masked_score = -1e30


def from_behind(block, axis, distance):
    devices = range(lax.axis_size(axis))
    route = [(i - distance, i) for i in devices if i - distance in devices]
    return lax.ppermute(block, axis, route)


def split_up(x, dim, peers):
    dims = x.shape
    tiles = x.reshape(*dims[:dim], peers, dims[dim] // peers, *dims[dim + 1 :])
    return jnp.moveaxis(tiles, dim, 0)


def sum_at_owner(x, axis, dim):
    tiles = split_up(x, dim, lax.axis_size(axis))
    arrived = lax.all_to_all(tiles, axis, split_axis=0, concat_axis=0, tiled=True)
    return arrived.astype(jnp.float32).sum(axis=0)


def side_by_side(arrays, axis, dim, along):
    widths = [math.prod(a.shape[along:]) for a in arrays]
    both = jnp.concatenate(
        [a.reshape(*a.shape[:along], w) for a, w in zip(arrays, widths)], axis=along
    )
    whole = sum_at_owner(both, axis, dim)
    tiles = jnp.split(whole, [sum(widths[:k]) for k in range(1, len(widths))], axis=along)
    return tuple((b.reshape(*whole.shape[:along], *a.shape[along:]) for a, b in zip(arrays, tiles)))


def gelu_exact(values):
    return jax.nn.gelu(values, approximate=False)


def row_scale(values):
    return lax.rsqrt(jnp.mean(values * values, axis=-1, keepdims=True) + epsilon)


def norm_backward(incoming, normal_hat, row_factor, gain):
    scaled = incoming * gain
    inner = jnp.mean(scaled * normal_hat, axis=-1, keepdims=True)
    return (row_factor * (scaled - normal_hat * inner), jnp.sum(incoming * normal_hat, axis=0))


def parent_of(seg_ids, parents):
    seg_table = jnp.arange(parents.shape[0], dtype=jnp.int32)
    hits = seg_ids[:, None] == seg_table[None, :]
    return jnp.sum(jnp.where(hits, parents[None, :], 0), axis=1)


def shards(
    layer_input,
    cotangent,
    segments,
    parents,
    norm1_gain,
    w_query,
    w_key,
    w_value,
    w_out,
    norm2_gain,
    w_up,
    w_down,
):
    gain_one, full_query, full_key, full_value, full_out, gain_two, full_up, full_down = (
        lax.all_gather(norm1_gain, "dp", axis=0, tiled=True),
        lax.all_gather(w_query, "dp", axis=0, tiled=True),
        lax.all_gather(w_key, "dp", axis=0, tiled=True),
        lax.all_gather(w_value, "dp", axis=0, tiled=True),
        lax.all_gather(w_out, "dp", axis=1, tiled=True),
        lax.all_gather(norm2_gain, "dp", axis=0, tiled=True),
        lax.all_gather(w_up, "dp", axis=0, tiled=True),
        lax.all_gather(w_down, "dp", axis=1, tiled=True),
    )
    gain_one = gain_one.astype(jnp.float32)
    gain_two = gain_two.astype(jnp.float32)
    row_count = layer_input.shape[0]
    token_count = row_count * lax.axis_size("tensor")
    position = lax.axis_index("dp") * token_count
    head_width = full_query.shape[1]
    head_count = head_width // HD
    scaling = HD ** (-0.5)
    block_rows = min(640, token_count)
    block_count = token_count // block_rows
    span = WINDOW + block_rows
    hop_count = (WINDOW + token_count - 1) // token_count
    inputs = layer_input.astype(jnp.float32)
    factor_one = row_scale(inputs)
    hat_one = inputs * factor_one
    normed = (hat_one * gain_one).astype(jnp.bfloat16)
    normed_all = lax.all_gather(normed, "tensor", axis=0, tiled=True)
    queries = jnp.dot(normed_all, full_query, preferred_element_type=jnp.float32).astype(
        jnp.bfloat16
    )
    keys_own = jnp.dot(normed_all, full_key, preferred_element_type=jnp.float32).astype(
        jnp.bfloat16
    )
    values_own = jnp.dot(normed_all, full_value, preferred_element_type=jnp.float32).astype(
        jnp.bfloat16
    )
    pair_own = jnp.concatenate([keys_own, values_own], axis=1)
    halo_parts = []
    for distance in range(1, hop_count + 1):
        length = min(token_count, WINDOW - (distance - 1) * token_count)
        piece = pair_own[token_count - length :]
        moved = from_behind(piece, "dp", distance)
        halo_parts.append(moved)
    pair_all = jnp.concatenate(halo_parts[::-1] + [pair_own], axis=0)
    seg_padded = jnp.concatenate([jnp.full((WINDOW,), -1, jnp.int32), segments])
    seg_keys = lax.dynamic_slice_in_dim(seg_padded, position, WINDOW + token_count, 0)
    seg_query = seg_keys[WINDOW:]
    parent_one = parent_of(seg_query, parents)
    parent_two = parent_of(parent_one, parents)
    query_spots = jnp.arange(block_rows, dtype=jnp.int32)
    key_spots = jnp.arange(span, dtype=jnp.int32)

    def scores_of(offset):
        query_block = lax.dynamic_slice_in_dim(queries, offset, block_rows, 0).reshape(
            block_rows, head_count, HD
        )
        pair_block = lax.dynamic_slice_in_dim(pair_all, offset, span, 0)
        key_block = pair_block[:, :head_width].reshape(span, head_count, HD)
        value_block = pair_block[:, head_width:].reshape(span, head_count, HD)
        own_seg = lax.dynamic_slice_in_dim(seg_query, offset, block_rows, 0)
        up_one = lax.dynamic_slice_in_dim(parent_one, offset, block_rows, 0)
        up_two = lax.dynamic_slice_in_dim(parent_two, offset, block_rows, 0)
        near_seg = lax.dynamic_slice_in_dim(seg_keys, offset, span, 0)
        gap = WINDOW + query_spots[:, None] - key_spots[None, :]
        same_path = (
            (near_seg[None, :] == own_seg[:, None])
            | (near_seg[None, :] == up_one[:, None])
            | (near_seg[None, :] == up_two[:, None])
        )
        allowed = (gap >= 0) & (gap < WINDOW) & same_path
        raw = (
            jnp.einsum("qhd,khd->hqk", query_block, key_block, preferred_element_type=jnp.float32)
            * scaling
        )
        return (jnp.where(allowed[None], raw, masked_score), query_block, key_block, value_block)

    def forward_block(block_index):
        scores, query_block, key_block, value_block = scores_of(block_index * block_rows)
        row_max = jnp.max(scores, axis=-1, keepdims=True)
        exponent = jnp.exp(scores - row_max)
        denominator = jnp.sum(exponent, axis=-1, keepdims=True)
        weights = (exponent / denominator).astype(jnp.bfloat16)
        mixed = jnp.einsum("hqk,khd->qhd", weights, value_block, preferred_element_type=jnp.float32)
        return (
            mixed.reshape(block_rows, head_width).astype(jnp.bfloat16),
            (row_max + jnp.log(denominator))[..., 0],
        )

    context_blocks, logsum_blocks = lax.map(forward_block, jnp.arange(block_count, dtype=jnp.int32))
    context = context_blocks.reshape(token_count, head_width)
    middle = inputs + lax.psum_scatter(
        jnp.dot(context, full_out, preferred_element_type=jnp.float32).astype(jnp.bfloat16),
        "tensor",
        scatter_dimension=0,
        tiled=True,
    ).astype(jnp.float32)
    factor_two = row_scale(middle)
    hat_two = middle * factor_two
    normed_two = (hat_two * gain_two).astype(jnp.bfloat16)
    normed_two_all = lax.all_gather(normed_two, "tensor", axis=0, tiled=True)
    upper = jnp.dot(normed_two_all, full_up, preferred_element_type=jnp.float32)
    active = gelu_exact(upper).astype(jnp.bfloat16)
    result = middle + lax.psum_scatter(
        jnp.dot(active, full_down, preferred_element_type=jnp.float32).astype(jnp.bfloat16),
        "tensor",
        scatter_dimension=0,
        tiled=True,
    ).astype(jnp.float32)
    incoming = cotangent.astype(jnp.float32)
    incoming_all = lax.all_gather(cotangent, "tensor", axis=0, tiled=True)
    grad_down = jnp.einsum("tf,td->fd", active, incoming_all, preferred_element_type=jnp.float32)
    grad_active = jnp.einsum(
        "td,fd->tf", incoming_all, full_down, preferred_element_type=jnp.float32
    )
    unused_value, gelu_pull = jax.vjp(gelu_exact, upper)
    grad_upper = gelu_pull(grad_active)[0].astype(jnp.bfloat16)
    grad_up = jnp.einsum(
        "tc,tf->cf", normed_two_all, grad_upper, preferred_element_type=jnp.float32
    )
    grad_normed_two = lax.psum_scatter(
        jnp.einsum("tf,cf->tc", grad_upper, full_up, preferred_element_type=jnp.float32).astype(
            jnp.bfloat16
        ),
        "tensor",
        scatter_dimension=0,
        tiled=True,
    ).astype(jnp.float32)
    through_two, gain_two_part = norm_backward(grad_normed_two, hat_two, factor_two, gain_two)
    grad_middle = incoming + through_two
    grad_middle_all = lax.all_gather(grad_middle.astype(jnp.bfloat16), "tensor", axis=0, tiled=True)
    grad_out = jnp.einsum("tc,td->cd", context, grad_middle_all, preferred_element_type=jnp.float32)
    grad_context = jnp.einsum(
        "td,cd->tc", grad_middle_all, full_out, preferred_element_type=jnp.float32
    ).astype(jnp.bfloat16)

    def backward_block(block_index, carry):
        grad_queries, grad_pairs = carry
        offset = block_index * block_rows
        scores, query_block, key_block, value_block = scores_of(offset)
        logsum = lax.dynamic_index_in_dim(logsum_blocks, block_index, 0, keepdims=False)
        probs = jnp.exp(scores - logsum[..., None])
        grad_rows = lax.dynamic_slice_in_dim(grad_context, offset, block_rows, 0).reshape(
            block_rows, head_count, HD
        )
        grad_probs = jnp.einsum(
            "qhd,khd->hqk", grad_rows, value_block, preferred_element_type=jnp.float32
        )
        inner = jnp.sum(probs * grad_probs, axis=-1, keepdims=True)
        grad_scores = (probs * (grad_probs - inner)).astype(jnp.bfloat16)
        grad_query_block = (
            jnp.einsum("hqk,khd->qhd", grad_scores, key_block, preferred_element_type=jnp.float32)
            * scaling
        )
        grad_key_block = (
            jnp.einsum("hqk,qhd->khd", grad_scores, query_block, preferred_element_type=jnp.float32)
            * scaling
        )
        grad_value_block = jnp.einsum(
            "hqk,qhd->khd",
            probs.astype(jnp.bfloat16),
            grad_rows,
            preferred_element_type=jnp.float32,
        )
        grad_queries = lax.dynamic_update_slice_in_dim(
            grad_queries, grad_query_block.reshape(block_rows, head_width), offset, 0
        )
        update = jnp.concatenate(
            [grad_key_block.reshape(span, head_width), grad_value_block.reshape(span, head_width)],
            axis=1,
        )
        current = lax.dynamic_slice_in_dim(grad_pairs, offset, span, 0)
        grad_pairs = lax.dynamic_update_slice_in_dim(grad_pairs, current + update, offset, 0)
        return (grad_queries, grad_pairs)

    start_carry = (
        jnp.zeros((token_count, head_width), jnp.float32),
        jnp.zeros((WINDOW + token_count, 2 * head_width), jnp.float32),
    )
    grad_queries, grad_pairs = lax.fori_loop(0, block_count, backward_block, start_carry)
    grad_own = grad_pairs[WINDOW:]
    for distance in range(1, hop_count + 1):
        length = min(token_count, WINDOW - (distance - 1) * token_count)
        first_row = WINDOW - (distance - 1) * token_count - length
        piece = grad_pairs[first_row : first_row + length]
        returned = from_behind(piece.astype(jnp.bfloat16), "dp", -distance).astype(piece.dtype)
        grad_own = grad_own + jnp.pad(returned, ((token_count - length, 0), (0, 0)))
    grad_keys = grad_own[:, :head_width].astype(jnp.bfloat16)
    grad_values = grad_own[:, head_width:].astype(jnp.bfloat16)
    grad_queries_low = grad_queries.astype(jnp.bfloat16)
    grad_query = jnp.einsum(
        "tc,tq->cq", normed_all, grad_queries_low, preferred_element_type=jnp.float32
    )
    grad_key = jnp.einsum("tc,tq->cq", normed_all, grad_keys, preferred_element_type=jnp.float32)
    grad_value = jnp.einsum(
        "tc,tq->cq", normed_all, grad_values, preferred_element_type=jnp.float32
    )
    part_query = jnp.einsum(
        "tq,cq->tc", grad_queries_low, full_query, preferred_element_type=jnp.float32
    )
    part_key = jnp.einsum("tq,cq->tc", grad_keys, full_key, preferred_element_type=jnp.float32)
    part_value = jnp.einsum(
        "tq,cq->tc", grad_values, full_value, preferred_element_type=jnp.float32
    )
    grad_normed = lax.psum_scatter(
        (part_query + part_key + part_value).astype(jnp.bfloat16),
        "tensor",
        scatter_dimension=0,
        tiled=True,
    ).astype(jnp.float32)
    through_one, gain_one_part = norm_backward(grad_normed, hat_one, factor_one, gain_one)
    grad_inputs = grad_middle + through_one
    gain_one_sum, gain_two_sum = lax.psum((gain_one_part, gain_two_part), "tensor")
    summed = (
        *side_by_side(
            (
                gain_one_sum.astype(jnp.bfloat16),
                grad_query.astype(jnp.bfloat16),
                grad_key.astype(jnp.bfloat16),
                grad_value.astype(jnp.bfloat16),
            ),
            "dp",
            0,
            1,
        ),
        sum_at_owner(grad_out.astype(jnp.bfloat16), "dp", 1),
        *side_by_side(
            (gain_two_sum.astype(jnp.bfloat16), grad_up.astype(jnp.bfloat16)), "dp", 0, 1
        ),
        sum_at_owner(grad_down.astype(jnp.bfloat16), "dp", 1),
    )
    return (
        result.astype(jnp.bfloat16),
        grad_inputs.astype(jnp.bfloat16),
        summed[0],
        summed[1],
        summed[2],
        summed[3],
        summed[4],
        summed[5],
        summed[6],
        summed[7],
    )


def solution(mesh):
    return jax.shard_map(
        shards,
        mesh=mesh,
        in_specs=(
            P(("dp", "tensor"), None),
            P(("dp", "tensor"), None),
            P(),
            P(),
            P("dp"),
            P("dp", "tensor"),
            P("dp", "tensor"),
            P("dp", "tensor"),
            P("tensor", "dp"),
            P("dp"),
            P("dp", "tensor"),
            P("tensor", "dp"),
        ),
        out_specs=(
            P(("dp", "tensor"), None),
            P(("dp", "tensor"), None),
            P("dp"),
            P("dp", "tensor"),
            P("dp", "tensor"),
            P("dp", "tensor"),
            P("tensor", "dp"),
            P("dp"),
            P("dp", "tensor"),
            P("tensor", "dp"),
        ),
        check_vma=False,
    )
```

profile of v0, /device:TPU:0, one launch (start us, length us, event | category | flops | bytes accessed | tf_op | source)
XLA Modules:
  0.0 772.6 jit_solution(16327131825716059331)
XLA Ops:
  12.9 23.7 %all-reduce.5 = (bf16[768]{0:T(1024)(128)(2,1)S(1)}, bf16[768]{0:T(1024)(128)(2,1)}) all-reduce(bf16[768]{0:T(1024)(128)(2,1)S(1)} %dynamic-update-slice, bf16[768]{0:T(1024)(128)(2,1)S(1)} %dynamic-update-slice.1), channel_id=1, replica_groups=mesh['dp'=8,'tensor'=4] {'dp'}, use_global_device_ids=true, to_apply=%add.2 | all-reduce | flops 1536 | bytes 6144
  41.0 31.2 %all_gather.38 = bf16[768,192]{1,0:T(8,128)(2,1)S(1)} all-gather(bf16[96,192]{1,0:T(8,128)(2,1)} %param.22), channel_id=1, replica_groups=mesh['dp'=8,'tensor'=4] {'dp'}, dimensions={0}, use_global_device_ids=true | all-gather | bytes 331776 | tf_op jit(solution)/shard_map/all_gather | solution.py:78
  72.2 31.2 %all_gather.39 = bf16[768,192]{1,0:T(8,128)(2,1)S(1)} all-gather(bf16[96,192]{1,0:T(8,128)(2,1)} %param.23), channel_id=1, replica_groups=mesh['dp'=8,'tensor'=4] {'dp'}, dimensions={0}, use_global_device_ids=true | all-gather | bytes 331776 | tf_op jit(solution)/shard_map/all_gather | solution.py:79
  110.2 46.0 %all_gather.41 = bf16[192,768]{0,1:T(8,128)(2,1)} all-gather(bf16[192,96]{0,1:T(8,128)(2,1)S(1)} %copy.48), channel_id=1, replica_groups=mesh['dp'=8,'tensor'=4] {'dp'}, dimensions={1}, use_global_device_ids=true | all-gather | bytes 331776 | tf_op jit(solution)/shard_map/all_gather | solution.py:80
  156.2 31.0 %all_gather.40 = bf16[768,192]{1,0:T(8,128)(2,1)S(1)} all-gather(bf16[96,192]{1,0:T(8,128)(2,1)S(1)} %copy-done.35), channel_id=1, replica_groups=mesh['dp'=8,'tensor'=4] {'dp'}, dimensions={0}, use_global_device_ids=true | all-gather | bytes 331776 | tf_op jit(solution)/shard_map/all_gather | solution.py:77
  193.2 72.5 %while.29 = (s32[]{:T(128)}, bf16[2,640,192]{1,2,0:T(8,128)(2,1)}, f32[2,3,640]{2,1,0:T(4,128)S(1)}, s32[2]{0:T(128)S(1)}, bf16[2816,384]{0,1:T(8,128)(2,1)}, /*...) while((s32[]{:T(128)}, bf16[2,640,192]{1,2,0:T(8,128)(2,1)}, ...), condition=%wide.region_6.7_spmd.clone, body=%wide.region_3.6_spmd.clone.sunk | while | flops 1133730560 | bytes 66249560 | solution.py:163
  195.0 4.8 fusion.135
  201.3 8.0 %fusion.136 = (f32[3,640]{1,0:T(4,128)S(1)}, f32[3,640,2176]{2,1,0:T(8,128)}) fusion(pred[640,2176]{1,0:T(8,128)(4,1)S(1)} %fusion.135, bf16[640,3,64]{0,2,1:T(8,128)(2,1)S(1)} %bitcast.146, bf16[2176,3,64]{0,2,1:T(8,128)(2,1)S(1)} %bitcast.145), kind=kOutput, calls=%fused_computation.7.clone.1 | convolution fusion | flops 547305600 | bytes 19193344 | tf_op jit(solution)/shard_map/while/body/eval_jaxpr/qhd,khd->hqk/dot_general | solution.py:146
  209.3 10.5 %fusion.137 = f32[3,640]{1,0:T(4,128)S(1)} fusion(f32[3,640,2176]{2,1,0:T(8,128)} %get-tuple-element.566, f32[3,640]{1,0:T(4,128)S(1)} %get-tuple-element.567, pred[640,2176]{1,0:T(8,128)(4,1)S(1)} %fusion.135), kind=kLoop, calls=%fused_computation.8.clone.1 | loop fusion | flops 16709760 | bytes 18119680 | tf_op jit(solution)/shard_map/while/body/eval_jaxpr/reduce_sum | solution.py:155
  219.8 8.8 %fusion.138 = bf16[3,64,640]{2,1,0:T(8,128)(2,1)S(1)} fusion(bf16[2176,3,64]{0,2,1:T(8,128)(2,1)S(1)} %bitcast.144, f32[3,640,2176]{2,1,0:T(8,128)} %get-tuple-element.566, f32[3,640]{1,0:T(4,128)S(1)} %fusion.137, f32[3,640]{1,0:T(4,128)S(1)} %get-tuple-element.567, pred[640,2176]{1,0:T(8,128)(4,1)S(1)} %fusion.135), kind=kOutput, calls=%fused_computation.15.clone.1 | convolution fusion | flops 555786240 | bytes 19201024 | tf_op jit(solution)/shard_map/while/body/eval_jaxpr/hqk,khd->qhd/dot_general | solution.py:157
  231.1 4.8 fusion.135
  237.5 8.0 %fusion.136 = (f32[3,640]{1,0:T(4,128)S(1)}, f32[3,640,2176]{2,1,0:T(8,128)}) fusion(pred[640,2176]{1,0:T(8,128)(4,1)S(1)} %fusion.135, bf16[640,3,64]{0,2,1:T(8,128)(2,1)S(1)} %bitcast.146, bf16[2176,3,64]{0,2,1:T(8,128)(2,1)S(1)} %bitcast.145), kind=kOutput, calls=%fused_computation.7.clone.1 | convolution fusion | flops 547305600 | bytes 19193344 | tf_op jit(solution)/shard_map/while/body/eval_jaxpr/qhd,khd->hqk/dot_general | solution.py:146
  245.5 10.5 %fusion.137 = f32[3,640]{1,0:T(4,128)S(1)} fusion(f32[3,640,2176]{2,1,0:T(8,128)} %get-tuple-element.566, f32[3,640]{1,0:T(4,128)S(1)} %get-tuple-element.567, pred[640,2176]{1,0:T(8,128)(4,1)S(1)} %fusion.135), kind=kLoop, calls=%fused_computation.8.clone.1 | loop fusion | flops 16709760 | bytes 18119680 | tf_op jit(solution)/shard_map/while/body/eval_jaxpr/reduce_sum | solution.py:155
  256.0 8.9 %fusion.138 = bf16[3,64,640]{2,1,0:T(8,128)(2,1)S(1)} fusion(bf16[2176,3,64]{0,2,1:T(8,128)(2,1)S(1)} %bitcast.144, f32[3,640,2176]{2,1,0:T(8,128)} %get-tuple-element.566, f32[3,640]{1,0:T(4,128)S(1)} %fusion.137, f32[3,640]{1,0:T(4,128)S(1)} %get-tuple-element.567, pred[640,2176]{1,0:T(8,128)(4,1)S(1)} %fusion.135), kind=kOutput, calls=%fused_computation.15.clone.1 | convolution fusion | flops 555786240 | bytes 19201024 | tf_op jit(solution)/shard_map/while/body/eval_jaxpr/hqk,khd->qhd/dot_general | solution.py:157
  271.0 32.7 %reduce-scatter.5.cloned.1.call-done = bf16[320,768]{1,0:T(8,128)(2,1)} async-done(((bf16[1280,768]{1,0:T(8,128)(2,1)}), bf16[320,768]{1,0:T(8,128)(2,1)}) %reduce-scatter.5.cloned.1.call-update) | async-done | bytes 491536 | tf_op jit(solution)/shard_map/reduce_scatter | solution.py:165
  308.4 8.9 %all-gather.11.cloned.1.call-done = bf16[768,768]{1,0:T(8,128)(2,1)} async-done(((bf16[96,768]{1,0:T(8,128)(2,1)}), bf16[768,768]{1,0:T(8,128)(2,1)}) %all-gather.11.cloned.1.call-update) | async-done | bytes 1179664 | tf_op jit(solution)/shard_map/all_gather | solution.py:82
  317.4 22.3 %all-gather.9.cloned.1.call-done = bf16[1280,768]{1,0:T(8,128)(2,1)} async-done(((bf16[320,768]{1,0:T(8,128)(2,1)}), bf16[1280,768]{1,0:T(8,128)(2,1)}) %all-gather.9.cloned.1.call-update) | async-done | bytes 1966096 | tf_op jit(solution)/shard_map/all_gather | solution.py:174
  339.7 5.5 fusion.64
  345.1 38.4 %all-gather.13.cloned.1.call-done = bf16[768,768]{0,1:T(8,128)(2,1)} async-done(((bf16[768,96]{0,1:T(8,128)(2,1)}), bf16[768,768]{0,1:T(8,128)(2,1)}) %all-gather.13.cloned.1.call-update) | async-done | bytes 1179664 | tf_op jit(solution)/shard_map/all_gather | solution.py:83
  383.5 21.9 %all-gather.15.cloned.1.call-done = bf16[1280,768]{1,0:T(8,128)(2,1)} async-done(((bf16[320,768]{1,0:T(8,128)(2,1)}), bf16[1280,768]{1,0:T(8,128)(2,1)}) %all-gather.15.cloned.1.call-update) | async-done | bytes 1966096 | tf_op jit(solution)/shard_map/all_gather | solution.py:184
  405.4 13.1 %add_convert_fusion = (bf16[1280,768]{1,0:T(8,128)(2,1)S(1)}, f32[1280,768]{1,0:T(8,128)}) fusion(f32[1280,768]{1,0:T(8,128)} %fusion.64, bf16[1280,768]{1,0:T(8,128)(2,1)} %all-gather.15.cloned.1.call-done, bf16[768,768]{0,1:T(8,128)(2,1)} %all-gather.13.cloned.1.call-done), kind=kOutput, calls=%fused_computation.47 | convolution fusion | flops 1580728320 | bytes 12976128 | tf_op jit(solution)/shard_map/td,fd->tf/dot_general | solution.py:186
  419.8 4.4 convolution_convert_fusion.1
  424.3 30.7 %reduce-scatter.9.cloned.1.call-done = bf16[320,768]{1,0:T(8,128)(2,1)} async-done(((bf16[1280,768]{1,0:T(8,128)(2,1)}), bf16[320,768]{1,0:T(8,128)(2,1)}) %reduce-scatter.9.cloned.1.call-update) | async-done | bytes 491536 | tf_op jit(solution)/shard_map/reduce_scatter | solution.py:194
  459.9 21.4 %all-gather.17.cloned.1.call-done = bf16[1280,768]{1,0:T(8,128)(2,1)} async-done(((bf16[320,768]{1,0:T(8,128)(2,1)}), bf16[1280,768]{1,0:T(8,128)(2,1)}) %all-gather.17.cloned.1.call-update) | async-done | bytes 1966096 | tf_op jit(solution)/shard_map/all_gather | solution.py:204
  487.6 112.6 %while.30 = (s32[]{:T(128)}, bf16[1280,192]{0,1:T(8,128)(2,1)}, f32[2816,384]{0,1:T(8,128)}, bf16[2816,384]{0,1:T(8,128)(2,1)}, s32[2816]{0:T(1024)S(1)}, /*inde...) while((s32[]{:T(128)}, bf16[1280,192]{0,1:T(8,128)(2,1)}, ...), condition=%wide.region_14.15_spmd.clone, body=%wide.region_12.14_spmd.clone.sunk | while | flops 2727729920 | bytes 220916592 | solution.py:253
  488.9 4.8 fusion.151
  495.2 8.1 %fusion.150 = f32[3,640,2176]{2,1,0:T(8,128)} fusion(bf16[640,3,64]{0,2,1:T(8,128)(2,1)S(1)} %bitcast.141, bf16[2176,3,64]{0,2,1:T(8,128)(2,1)S(1)} %bitcast.140), kind=kOutput, calls=%fused_computation.138.clone.1 | convolution fusion | flops 534773760 | bytes 17793024 | tf_op jit(solution)/shard_map/while/body/eval_jaxpr/qhd,khd->hqk/dot_general | solution.py:219
  503.3 15.1 %multiply_reduce_fusion.3 = (f32[3,640]{1,0:T(4,128)S(1)}, f32[3,640,2176]{2,1,0:T(8,128)}) fusion(f32[3,640,2176]{2,1,0:T(8,128)} %fusion.150, f32[3,640]{1,0:T(4,128)S(1)} %dynamic-slice_bitcast_fusion.2, bf16[640,3,64]{0,2,1:T(8,128)(2,1)S(1)} %bitcast.138, bf16[2176,3,64]{0,2,1:T(8,128)(2,1)S(1)} %bitcast.135, pred[640,2176]{1,0:T(8,128)(4,1)S(1)} %fusion.151), kind=kOutput, calls=%fused_computation.24.clone.1 | convolution fusion | flops 555661440 | bytes 35912704 | tf_op jit(solution)/shard_map/while/body/eval_jaxpr/qhd,khd->hqk/dot_general | solution.py:146
  518.5 11.4 %multiply_convert_fusion.4 = bf16[3,640,2176]{2,1,0:T(8,128)(2,1)S(1)} fusion(f32[3,640,2176]{2,1,0:T(8,128)} %get-tuple-element.583, f32[3,640,2176]{2,1,0:T(8,128)} %fusion.150, f32[3,640]{1,0:T(4,128)S(1)} %get-tuple-element.584), kind=kLoop, calls=%fused_computation.23.clone.1 | loop fusion | flops 12533760 | bytes 41786880 | tf_op jit(solution)/shard_map/while/body/eval_jaxpr/convert_element_type | solution.py:223
  529.9 3.9 copy-done
  539.5 4.4 fusion.153
  545.1 4.8 fusion.151
  551.5 8.1 %fusion.150 = f32[3,640,2176]{2,1,0:T(8,128)} fusion(bf16[640,3,64]{0,2,1:T(8,128)(2,1)S(1)} %bitcast.141, bf16[2176,3,64]{0,2,1:T(8,128)(2,1)S(1)} %bitcast.140), kind=kOutput, calls=%fused_computation.138.clone.1 | convolution fusion | flops 534773760 | bytes 17793024 | tf_op jit(solution)/shard_map/while/body/eval_jaxpr/qhd,khd->hqk/dot_general | solution.py:219
  559.6 15.1 %multiply_reduce_fusion.3 = (f32[3,640]{1,0:T(4,128)S(1)}, f32[3,640,2176]{2,1,0:T(8,128)}) fusion(f32[3,640,2176]{2,1,0:T(8,128)} %fusion.150, f32[3,640]{1,0:T(4,128)S(1)} %dynamic-slice_bitcast_fusion.2, bf16[640,3,64]{0,2,1:T(8,128)(2,1)S(1)} %bitcast.138, bf16[2176,3,64]{0,2,1:T(8,128)(2,1)S(1)} %bitcast.135, pred[640,2176]{1,0:T(8,128)(4,1)S(1)} %fusion.151), kind=kOutput, calls=%fused_computation.24.clone.1 | convolution fusion | flops 555661440 | bytes 35912704 | tf_op jit(solution)/shard_map/while/body/eval_jaxpr/qhd,khd->hqk/dot_general | solution.py:146
  574.7 11.4 %multiply_convert_fusion.4 = bf16[3,640,2176]{2,1,0:T(8,128)(2,1)S(1)} fusion(f32[3,640,2176]{2,1,0:T(8,128)} %get-tuple-element.583, f32[3,640,2176]{2,1,0:T(8,128)} %fusion.150, f32[3,640]{1,0:T(4,128)S(1)} %get-tuple-element.584), kind=kLoop, calls=%fused_computation.23.clone.1 | loop fusion | flops 12533760 | bytes 41786880 | tf_op jit(solution)/shard_map/while/body/eval_jaxpr/convert_element_type | solution.py:223
  586.1 3.9 copy-done
  595.7 4.4 fusion.153
  606.3 27.3 %collective-permute-done.3 = bf16[256,384]{0,1:T(8,128)(2,1)S(1)} collective-permute-done((bf16[256,384]{0,1:T(8,128)(2,1)S(1)}, bf16[256,384]{0,1:T(8,128)(2,1)S(1)}, u32[]{:S(2)}, u32[]{:S(2)}) %collective-permute-start.3) | collective-permute-done | bytes 196640 | tf_op jit(solution)/shard_map/ppermute | solution.py:16
  638.9 4.0 multiply_convert_fusion.1
  645.7 4.3 all-to-all-start.3
  650.0 4.3 convolution_convert_fusion.2
  667.0 11.4 %all-to-all-done.3 = bf16[8,768,96]{1,2,0:T(8,128)(2,1)} async-done(((bf16[8,768,96]{1,2,0:T(8,128)(2,1)}), bf16[8,768,96]{1,2,0:T(8,128)(2,1)}, u32[]{:S(2)}, u32[]{:S(2)}) %all-to-all-start.3) | async-done | bytes 1179680 | tf_op jit(solution)/shard_map/all_to_all | solution.py:27
  678.4 4.1 all-to-all-start.1
  686.5 6.5 all-reduce.4
  696.0 6.1 all-to-all-start
  702.2 4.9 convolution_convert_fusion.8
  710.6 15.5 %all-to-all-done = bf16[8,96,577]{2,1,0:T(8,128)(2,1)S(1)} async-done(((bf16[8,96,577]{2,1,0:T(8,128)(2,1)}), bf16[8,96,577]{2,1,0:T(8,128)(2,1)S(1)}, u32[]{:S(2)}, u32[]{:S(2)}) %all-to-all-start) | async-done | bytes 886304 | tf_op jit(solution)/shard_map/all_to_all | solution.py:27
  739.1 24.3 %all-to-all-done.2 = bf16[8,96,769]{2,1,0:T(8,128)(2,1)S(1)} async-done(((bf16[8,96,769]{2,1,0:T(8,128)(2,1)}), bf16[8,96,769]{2,1,0:T(8,128)(2,1)S(1)}, u32[]{:S(2)}, u32[]{:S(2)}) %all-to-all-start.2) | async-done | bytes 1181216 | tf_op jit(solution)/shard_map/all_to_all | solution.py:27
  (242 shorter events, 119.0 us)
Async XLA Ops:
  8.0 95.4 %all-gather.7.cloned.1.call-start = ((), (), s32[]{:S(2)}) async-start(), calls=%async_computation.8 | async-start | bytes 2457600 | tf_op jit(solution)/shard_map/all_gather | solution.py:101
  9.3 30.9 %copy-start.36 = (f32[320]{0:T(512)}, f32[320]{0:T(512)S(1)}, u32[]{:S(2)}) copy-start(f32[320]{0:T(512)S(1)} %add_rsqrt_fusion.1) | copy-start | bytes 3844
  39.2 264.5 %reduce-scatter.5.cloned.1.call-start = ((), (), s32[]{:S(2)}) async-start(), calls=%async_computation.9 | async-start | bytes 2457600 | tf_op jit(solution)/shard_map/reduce_scatter | solution.py:165
  72.2 36.3 %copy-start.19 = (bf16[768,192]{1,0:T(8,128)(2,1)}, bf16[768,192]{1,0:T(8,128)(2,1)S(1)}, u32[]{:S(2)}) copy-start(bf16[768,192]{1,0:T(8,128)(2,1)S(1)} %all_gather.38) | copy-start | bytes 884740
  103.4 52.9 %copy-start.21 = (bf16[768,192]{1,0:T(8,128)(2,1)}, bf16[768,192]{1,0:T(8,128)(2,1)S(1)}, u32[]{:S(2)}) copy-start(bf16[768,192]{1,0:T(8,128)(2,1)S(1)} %all_gather.39) | copy-start | bytes 884740
  103.4 6.6 copy-start.42
  103.4 52.9 %copy-start.35 = (bf16[96,192]{1,0:T(8,128)(2,1)S(1)}, bf16[96,192]{1,0:T(8,128)(2,1)}, u32[]{:S(2)}) copy-start(bf16[96,192]{1,0:T(8,128)(2,1)} %param.21) | copy-start | bytes 110596
  105.9 82.6 %copy-start.3 = (bf16[1280,768]{1,0:T(8,128)(2,1)S(1)}, bf16[1280,768]{1,0:T(8,128)(2,1)}, u32[]{:S(2)}) copy-start(bf16[1280,768]{1,0:T(8,128)(2,1)} %all-gather.7.cloned.1.call-done) | copy-start | bytes 5898244
  108.5 83.2 %collective-permute-start.1 = (bf16[1280,384]{0,1:T(8,128)(2,1)S(1)}, bf16[1280,384]{0,1:T(8,128)(2,1)S(1)}, u32[]{:S(2)}, u32[]{:S(2)}) collective-permute-start(bf16[1280,384]{0,1:T(8,128)(2,1)S(1)} %pad_maximum_fusion.1), channel_id=1, source_target_pairs={{0,4},{4,8},{8,12},{12,16},{16,20},{20,24},{24,28},{1,5},{5,9},{9,... | collective-permute-start | bytes 2949128 | tf_op jit(solution)/shard_map/ppermute | solution.py:16
  187.2 4.5 collective-permute-start
  219.8 8.9 %copy-start.26 = (bf16[2,640,192]{1,2,0:T(8,128)(2,1)S(1)}, bf16[2,640,192]{1,2,0:T(8,128)(2,1)}, u32[]{:S(2)}) copy-start(bf16[2,640,192]{1,2,0:T(8,128)(2,1)} %get-tuple-element.602) | copy-start | bytes 1474564 | tf_op jit(solution)/shard_map/while
  256.0 8.9 %copy-start.26 = (bf16[2,640,192]{1,2,0:T(8,128)(2,1)S(1)}, bf16[2,640,192]{1,2,0:T(8,128)(2,1)}, u32[]{:S(2)}) copy-start(bf16[2,640,192]{1,2,0:T(8,128)(2,1)} %get-tuple-element.602) | copy-start | bytes 1474564 | tf_op jit(solution)/shard_map/while
  265.7 38.0 %copy-start.1 = (bf16[320,768]{1,0:T(8,128)(2,1)S(1)}, bf16[320,768]{1,0:T(8,128)(2,1)}, u32[]{:S(2)}) copy-start(bf16[320,768]{1,0:T(8,128)(2,1)} %param.16) | copy-start | bytes 1474564
  266.9 40.2 %copy-start.10 = (bf16[2,24,8,640]{3,2,0,1:T(8,128)(2,1)}, bf16[2,24,8,640]{3,2,0,1:T(8,128)(2,1)S(1)}, u32[]{:S(2)}) copy-start(bf16[2,24,8,640]{3,2,0,1:T(8,128)(2,1)S(1)} %copy.67) | copy-start | bytes 1474564
  270.1 47.3 %all-gather.11.cloned.1.call-start = ((), (), s32[]{:S(2)}) async-start(), calls=%async_computation.11 | async-start | bytes 1327104 | tf_op jit(solution)/shard_map/all_gather | solution.py:82
  270.7 69.0 %all-gather.9.cloned.1.call-start = ((), (), s32[]{:S(2)}) async-start(), calls=%async_computation.10 | async-start | bytes 2457600 | tf_op jit(solution)/shard_map/all_gather | solution.py:174
  271.0 186.2 %copy-start.29 = (f32[768]{0:T(1024)}, f32[768]{0:T(1024)S(1)}, u32[]{:S(2)}) copy-start(f32[768]{0:T(1024)S(1)} %convert_element_type.159) | copy-start | bytes 9220
  305.0 152.2 %copy-start.33 = (f32[320]{0:T(512)}, f32[320]{0:T(512)S(1)}, u32[]{:S(2)}) copy-start(f32[320]{0:T(512)S(1)} %add_rsqrt_fusion) | copy-start | bytes 3844
  307.1 76.4 %all-gather.13.cloned.1.call-start = ((), (), s32[]{:S(2)}) async-start(), calls=%async_computation.12 | async-start | bytes 1327104 | tf_op jit(solution)/shard_map/all_gather | solution.py:83
  307.6 97.7 %all-gather.15.cloned.1.call-start = ((), (), s32[]{:S(2)}) async-start(), calls=%async_computation.14 | async-start | bytes 2457600 | tf_op jit(solution)/shard_map/all_gather | solution.py:184
  308.4 146.7 %reduce-scatter.9.cloned.1.call-start = ((), (), s32[]{:S(2)}) async-start(), calls=%async_computation.15 | async-start | bytes 2457600 | tf_op jit(solution)/shard_map/reduce_scatter | solution.py:194
  419.8 35.2 %copy-start.5 = (bf16[320,768]{1,0:T(8,128)(2,1)S(1)}, bf16[320,768]{1,0:T(8,128)(2,1)}, u32[]{:S(2)}) copy-start(bf16[320,768]{1,0:T(8,128)(2,1)} %reduce-scatter.5.cloned.1.call-done) | copy-start | bytes 1474564
  419.8 37.4 %copy-start.7 = (bf16[320,768]{1,0:T(8,128)(2,1)S(1)}, bf16[320,768]{1,0:T(8,128)(2,1)}, u32[]{:S(2)}) copy-start(bf16[320,768]{1,0:T(8,128)(2,1)} %param.17) | copy-start | bytes 1474564
  424.2 57.0 %copy-start.25 = (bf16[192,768]{0,1:T(8,128)(2,1)S(1)}, bf16[192,768]{0,1:T(8,128)(2,1)}, u32[]{:S(2)}) copy-start(bf16[192,768]{0,1:T(8,128)(2,1)} %all_gather.41) | copy-start | bytes 884740
  424.2 57.0 %all-gather.17.cloned.1.call-start = ((), (), s32[]{:S(2)}) async-start(), calls=%async_computation.16 | async-start | bytes 2457600 | tf_op jit(solution)/shard_map/all_gather | solution.py:204
  457.2 30.4 %copy-start.38 = (f32[320]{0:T(512)}, f32[320]{0:T(512)S(1)}, u32[]{:S(2)}) copy-start(f32[320]{0:T(512)S(1)} %broadcast_multiply_fusion.1) | copy-start | bytes 3844
  459.4 225.5 %reduce-scatter.11.cloned.1.call-start = ((), (), s32[]{:S(2)}) async-start(), calls=%async_computation.17 | async-start | bytes 2457600 | tf_op jit(solution)/shard_map/reduce_scatter | solution.py:278
  518.5 15.3 %copy-start = (f32[3,640,2176]{2,1,0:T(8,128)S(1)}, f32[3,640,2176]{2,1,0:T(8,128)}, u32[]{:S(2)}) copy-start(f32[3,640,2176]{2,1,0:T(8,128)} %get-tuple-element.583) | copy-start | bytes 50135044 | tf_op jit(solution)/shard_map/while
  574.7 15.3 %copy-start = (f32[3,640,2176]{2,1,0:T(8,128)S(1)}, f32[3,640,2176]{2,1,0:T(8,128)}, u32[]{:S(2)}) copy-start(f32[3,640,2176]{2,1,0:T(8,128)} %get-tuple-element.583) | copy-start | bytes 50135044 | tf_op jit(solution)/shard_map/while
  602.8 30.9 %collective-permute-start.2 = (bf16[1280,384]{0,1:T(8,128)(2,1)S(1)}, bf16[1280,384]{0,1:T(8,128)(2,1)S(1)}, u32[]{:S(2)}, u32[]{:S(2)}) collective-permute-start(bf16[1280,384]{0,1:T(8,128)(2,1)S(1)} %slice.58), channel_id=1, source_target_pairs={{4,0},{8,4},{12,8},{16,12},{20,16},{24,20},{28,24},{5,1},{9,5},{13... | collective-permute-start | bytes 2949128 | tf_op jit(solution)/shard_map/ppermute | solution.py:16
  604.3 29.4 %collective-permute-start.3 = (bf16[256,384]{0,1:T(8,128)(2,1)S(1)}, bf16[256,384]{0,1:T(8,128)(2,1)S(1)}, u32[]{:S(2)}, u32[]{:S(2)}) collective-permute-start(bf16[256,384]{0,1:T(8,128)(2,1)S(1)} %slice.59), channel_id=1, source_target_pairs={{8,0},{12,4},{16,8},{20,12},{24,16},{28,20},{9,1},{13,5},{17,9},{2... | collective-permute-start | bytes 589832 | tf_op jit(solution)/shard_map/ppermute | solution.py:16
  605.6 29.9 %copy-start.20 = (bf16[768,192]{1,0:T(8,128)(2,1)S(1)}, bf16[768,192]{1,0:T(8,128)(2,1)}, u32[]{:S(2)}) copy-start(bf16[768,192]{1,0:T(8,128)(2,1)} %copy-done.19) | copy-start | bytes 884740
  645.7 32.7 %all-to-all-start.3 = ((bf16[8,768,96]{1,2,0:T(8,128)(2,1)}), bf16[8,768,96]{1,2,0:T(8,128)(2,1)}, u32[]{:S(2)}, u32[]{:S(2)}) async-start(bf16[8,768,96]{1,2,0:T(8,128)(2,1)} %bitcast.154), calls=%async_computation.7 | async-start | bytes 2359296 | tf_op jit(solution)/shard_map/all_to_all | solution.py:27
  650.0 84.5 %reduce-scatter.7.cloned.1.call-start = ((), (), s32[]{:S(2)}) async-start(), calls=%async_computation.13 | async-start | bytes 2457600 | tf_op jit(solution)/shard_map/reduce_scatter | solution.py:177
  658.6 23.9 %copy-start.18 = (bf16[1280,384]{0,1:T(8,128)(2,1)S(1)}, bf16[1280,384]{0,1:T(8,128)(2,1)}, u32[]{:S(2)}) copy-start(bf16[1280,384]{0,1:T(8,128)(2,1)} %copy-done.17) | copy-start | bytes 2949124
  662.8 22.2 %copy-start.2 = (bf16[320,768]{1,0:T(8,128)(2,1)S(1)}, bf16[320,768]{1,0:T(8,128)(2,1)}, u32[]{:S(2)}) copy-start(bf16[320,768]{1,0:T(8,128)(2,1)} %param.16) | copy-start | bytes 1474564
  662.8 22.2 %copy-start.32 = (f32[768]{0:T(1024)S(1)}, f32[768]{0:T(1024)}, u32[]{:S(2)}) copy-start(f32[768]{0:T(1024)} %copy-done.31) | copy-start | bytes 9220
  662.8 22.2 %copy-start.37 = (f32[320]{0:T(512)S(1)}, f32[320]{0:T(512)}, u32[]{:S(2)}) copy-start(f32[320]{0:T(512)} %copy-done.36) | copy-start | bytes 3844
  662.8 23.7 %copy-start.40 = (f32[768]{0:T(1024)S(1)}, f32[768]{0:T(1024)}, u32[]{:S(2)}) copy-start(f32[768]{0:T(1024)} %get-tuple-element.370) | copy-start | bytes 9220
  678.4 17.6 %all-to-all-start.1 = ((bf16[8,192,96]{2,1,0:T(8,128)(2,1)}), bf16[8,192,96]{2,1,0:T(8,128)(2,1)}, u32[]{:S(2)}, u32[]{:S(2)}) async-start(bf16[8,192,96]{2,1,0:T(8,128)(2,1)} %bitcast.150), calls=%async_computation.5 | async-start | bytes 786432 | tf_op jit(solution)/shard_map/all_to_all | solution.py:27
  696.0 30.0 %all-to-all-start = ((bf16[8,96,577]{2,1,0:T(8,128)(2,1)}), bf16[8,96,577]{2,1,0:T(8,128)(2,1)S(1)}, u32[]{:S(2)}, u32[]{:S(2)}) async-start(bf16[8,96,577]{2,1,0:T(8,128)(2,1)} %pad_maximum_fusion.2), calls=%async_computation.4 | async-start | bytes 1966080 | tf_op jit(solution)/shard_map/all_to_all | solution.py:27
  707.1 27.4 %copy-start.6 = (bf16[320,768]{1,0:T(8,128)(2,1)S(1)}, bf16[320,768]{1,0:T(8,128)(2,1)}, u32[]{:S(2)}) copy-start(bf16[320,768]{1,0:T(8,128)(2,1)} %reduce-scatter.5.cloned.1.call-done) | copy-start | bytes 1474564
  707.1 27.4 %copy-start.8 = (bf16[320,768]{1,0:T(8,128)(2,1)S(1)}, bf16[320,768]{1,0:T(8,128)(2,1)}, u32[]{:S(2)}) copy-start(bf16[320,768]{1,0:T(8,128)(2,1)} %param.17) | copy-start | bytes 1474564
  707.1 27.4 %copy-start.9 = (bf16[320,768]{1,0:T(8,128)(2,1)S(1)}, bf16[320,768]{1,0:T(8,128)(2,1)}, u32[]{:S(2)}) copy-start(bf16[320,768]{1,0:T(8,128)(2,1)} %reduce-scatter.9.cloned.1.call-done) | copy-start | bytes 1474564
  707.1 27.4 %copy-start.30 = (f32[768]{0:T(1024)S(1)}, f32[768]{0:T(1024)}, u32[]{:S(2)}) copy-start(f32[768]{0:T(1024)} %copy-done.29) | copy-start | bytes 9220
  707.1 27.4 %copy-start.34 = (f32[320]{0:T(512)S(1)}, f32[320]{0:T(512)}, u32[]{:S(2)}) copy-start(f32[320]{0:T(512)} %copy-done.33) | copy-start | bytes 3844
  707.1 27.4 %copy-start.39 = (f32[320]{0:T(512)S(1)}, f32[320]{0:T(512)}, u32[]{:S(2)}) copy-start(f32[320]{0:T(512)} %copy-done.38) | copy-start | bytes 3844
  727.0 36.4 %all-to-all-start.2 = ((bf16[8,96,769]{2,1,0:T(8,128)(2,1)}), bf16[8,96,769]{2,1,0:T(8,128)(2,1)S(1)}, u32[]{:S(2)}, u32[]{:S(2)}) async-start(bf16[8,96,769]{2,1,0:T(8,128)(2,1)} %pad_maximum_fusion), calls=%async_computation.6 | async-start | bytes 2752512 | tf_op jit(solution)/shard_map/all_to_all | solution.py:27
  (20 other events, 61.3 us)
Sparse Core Ops, SparseCore 0:
  39.3 19.0 all-gather.6
  270.2 33.4 reduce-scatter.4
  424.4 30.6 reduce-scatter.8
  639.0 28.7 reduce-scatter.10
  670.4 30.8 reduce-scatter.6
Sparse Core Ops, SparseCore 1:
  273.0 44.3 all-gather.10
  319.5 20.1 all-gather.8
  342.0 41.5 all-gather.12
  385.2 20.1 all-gather.14
  459.5 21.7 all-gather.16
where the time goes:
time: 778 us; the launch traced here: 773 us
  waiting for transfers between devices  259 us (33%)
  blocking collectives  170 us (22%)
  matrix products  150 us (19%)
  other arithmetic  107 us (14%)
  local copies, waits for them, and re-layouts  43.4 us (6%)
  starting transfers between devices  24.5 us (3%)
  between operations  17 us (2%)
    all_to_all x4, waiting for transfers between devices, sum_at_owner(): lax.all_to_all(tiles, axis, split_axis=0, concat_axis=0, tiled=True)  51.2 us
    dot_general x4, matrix products, scores_of(): jnp.einsum('qhd,khd->hqk', query_block, key_block, preferred_element_type...  46.3 us
    all_gather x1, blocking collectives, shards(): lax.all_gather(w_out, 'dp', axis=1, tiled=True)  46 us
    all_gather x1, waiting for transfers between devices, shards(): lax.all_gather(w_down, 'dp', axis=1, tiled=True)  38.4 us
    reduce_scatter x1, waiting for transfers between devices, shards(): lax.psum_scatter(jnp.dot(context, full_out, preferred_element_type=jnp.fl...  32.7 us
    all_gather x1, blocking collectives, shards(): lax.all_gather(w_key, 'dp', axis=0, tiled=True)  31.2 us
    all_gather x1, blocking collectives, shards(): lax.all_gather(w_value, 'dp', axis=0, tiled=True)  31.2 us
    all_gather x1, blocking collectives, shards(): lax.all_gather(w_query, 'dp', axis=0, tiled=True)  31 us
  transfers between devices with their start and end apart: 18, of which 12 were waited for; matrix products, arithmetic and copies ran while one was open for 8% of the time, Pallas kernels for 0%

commit v1 on v0

--- a/solution.py
+++ b/solution.py
@@ -8,6 +8,22 @@
 WINDOW = 1536
 epsilon = 1e-06
 masked_score = -1e30
+
+
+def collect(x, axis, dim):
+    ways, here, step = (lax.axis_size(axis), lax.axis_index(axis), x.shape[dim])
+    shape = [n * ways if d == dim else n for d, n in enumerate(x.shape)]
+    full = lax.dynamic_update_slice_in_dim(jnp.zeros(shape, x.dtype), x, here * step, axis=dim)
+    going_up = going_down = x
+    for far in range(1, ways // 2 + 1):
+        going_up = lax.ppermute(going_up, axis, [(d, (d + 1) % ways) for d in range(ways)])
+        full = lax.dynamic_update_slice_in_dim(full, going_up, (here - far) % ways * step, axis=dim)
+        if 2 * far < ways:
+            going_down = lax.ppermute(going_down, axis, [(d, (d - 1) % ways) for d in range(ways)])
+            full = lax.dynamic_update_slice_in_dim(
+                full, going_down, (here + far) % ways * step, axis=dim
+            )
+    return full
 
 
 def from_behind(block, axis, distance):
@@ -171,7 +187,7 @@
     factor_two = row_scale(middle)
     hat_two = middle * factor_two
     normed_two = (hat_two * gain_two).astype(jnp.bfloat16)
-    normed_two_all = lax.all_gather(normed_two, "tensor", axis=0, tiled=True)
+    normed_two_all = collect(normed_two, "tensor", 0)
     upper = jnp.dot(normed_two_all, full_up, preferred_element_type=jnp.float32)
     active = gelu_exact(upper).astype(jnp.bfloat16)
     result = middle + lax.psum_scatter(

time: 778 us -> 753 us (0.968)
  waiting for transfers between devices: 259 us -> 230 us
    all_gather x1 -> x0, waiting for transfers between devices: 22.3 us -> none  [shards(): normed_two_all = lax.all_gather(normed_two, 'tensor', axis=0, tiled=True)]
    ppermute x0 -> x3, waiting for transfers between devices: none -> 17.8 us  [the longest x2 17.8 us: collect(): lax.ppermute(going_up, axis, [(d, (d + 1) % ways) for d in range(ways)])]
    all_gather x1, waiting for transfers between devices: 38.4 us -> 24 us  [shards(): lax.all_gather(w_down, 'dp', axis=1, tiled=True)]
    all_gather x1, waiting for transfers between devices: 8.94 us -> 0.01 us  [shards(): lax.all_gather(w_up, 'dp', axis=0, tiled=True)]
  transfers between devices with their start and end apart: 18 -> 20, of which waited for: 12 -> 12; matrix products, arithmetic and copies ran while one was open for 8% -> 8% of each run, Pallas kernels for 0% -> 0%
where the time goes in v1:
time: 753 us; the launch traced here: 748 us
  waiting for transfers between devices  230 us (31%)
  blocking collectives  170 us (23%)
  matrix products  150 us (20%)
  other arithmetic  107 us (14%)
  local copies, waits for them, and re-layouts  47.3 us (6%)
  starting transfers between devices  26.2 us (3%)
  between operations  16.8 us (2%)
    all_to_all x4, waiting for transfers between devices, sum_at_owner(): lax.all_to_all(tiles, axis, split_axis=0, concat_axis=0, tiled=True)  51.1 us
    dot_general x4, matrix products, scores_of(): jnp.einsum('qhd,khd->hqk', query_block, key_block, preferred_element_type...  46.2 us
    all_gather x1, blocking collectives, shards(): lax.all_gather(w_out, 'dp', axis=1, tiled=True)  46 us
    reduce_scatter x1, waiting for transfers between devices, shards(): lax.psum_scatter(jnp.dot(context, full_out, preferred_element_type=jnp.fl...  31.6 us
    all_gather x1, blocking collectives, shards(): lax.all_gather(w_key, 'dp', axis=0, tiled=True)  31.2 us
    all_gather x1, blocking collectives, shards(): lax.all_gather(w_value, 'dp', axis=0, tiled=True)  31.2 us
    all_gather x1, blocking collectives, shards(): lax.all_gather(w_query, 'dp', axis=0, tiled=True)  31 us
    reduce_scatter x1, waiting for transfers between devices, shards(): lax.psum_scatter(jnp.einsum('tf,cf->tc', grad_upper, full_up, preferred_e...  30.7 us
  transfers between devices with their start and end apart: 20, of which 12 were waited for; matrix products, arithmetic and copies ran while one was open for 8% of the time, Pallas kernels for 0%

profile of v1, /device:TPU:0, one launch (start us, length us, event | category | flops | bytes accessed | tf_op | source)
XLA Modules:
  0.0 747.6 jit_solution(17046863699323357800)
XLA Ops:
  12.9 23.7 %all-reduce.5 = (bf16[768]{0:T(1024)(128)(2,1)S(1)}, bf16[768]{0:T(1024)(128)(2,1)}) all-reduce(bf16[768]{0:T(1024)(128)(2,1)S(1)} %dynamic-update-slice, bf16[768]{0:T(1024)(128)(2,1)S(1)} %dynamic-update-slice.1), channel_id=1, replica_groups=mesh['dp'=8,'tensor'=4] {'dp'}, use_global_device_ids=true, to_apply=%add.2 | all-reduce | flops 1536 | bytes 6144
  41.0 31.2 %all_gather.35 = bf16[768,192]{1,0:T(8,128)(2,1)S(1)} all-gather(bf16[96,192]{1,0:T(8,128)(2,1)} %param.22), channel_id=1, replica_groups=mesh['dp'=8,'tensor'=4] {'dp'}, dimensions={0}, use_global_device_ids=true | all-gather | bytes 331776 | tf_op jit(solution)/shard_map/all_gather | solution.py:94
  72.2 31.2 %all_gather.36 = bf16[768,192]{1,0:T(8,128)(2,1)S(1)} all-gather(bf16[96,192]{1,0:T(8,128)(2,1)} %param.23), channel_id=1, replica_groups=mesh['dp'=8,'tensor'=4] {'dp'}, dimensions={0}, use_global_device_ids=true | all-gather | bytes 331776 | tf_op jit(solution)/shard_map/all_gather | solution.py:95
  110.2 46.0 %all_gather.38 = bf16[192,768]{0,1:T(8,128)(2,1)} all-gather(bf16[192,96]{0,1:T(8,128)(2,1)S(1)} %copy.48), channel_id=1, replica_groups=mesh['dp'=8,'tensor'=4] {'dp'}, dimensions={1}, use_global_device_ids=true | all-gather | bytes 331776 | tf_op jit(solution)/shard_map/all_gather | solution.py:96
  156.2 31.0 %all_gather.37 = bf16[768,192]{1,0:T(8,128)(2,1)S(1)} all-gather(bf16[96,192]{1,0:T(8,128)(2,1)S(1)} %copy-done.36), channel_id=1, replica_groups=mesh['dp'=8,'tensor'=4] {'dp'}, dimensions={0}, use_global_device_ids=true | all-gather | bytes 331776 | tf_op jit(solution)/shard_map/all_gather | solution.py:93
  193.2 72.4 %while.29 = (s32[]{:T(128)}, bf16[2,640,192]{1,2,0:T(8,128)(2,1)}, f32[2,3,640]{2,1,0:T(4,128)S(1)}, s32[2]{0:T(128)S(1)}, bf16[2816,384]{0,1:T(8,128)(2,1)}, /*...) while((s32[]{:T(128)}, bf16[2,640,192]{1,2,0:T(8,128)(2,1)}, ...), condition=%wide.region_6.7_spmd.clone, body=%wide.region_3.6_spmd.clone.sunk | while | flops 1133730560 | bytes 66249560 | solution.py:179
  195.0 4.8 fusion.135
  201.3 8.0 %fusion.136 = (f32[3,640]{1,0:T(4,128)S(1)}, f32[3,640,2176]{2,1,0:T(8,128)}) fusion(pred[640,2176]{1,0:T(8,128)(4,1)S(1)} %fusion.135, bf16[640,3,64]{0,2,1:T(8,128)(2,1)S(1)} %bitcast.146, bf16[2176,3,64]{0,2,1:T(8,128)(2,1)S(1)} %bitcast.145), kind=kOutput, calls=%fused_computation.7.clone.1 | convolution fusion | flops 547305600 | bytes 19193344 | tf_op jit(solution)/shard_map/while/body/eval_jaxpr/qhd,khd->hqk/dot_general | solution.py:162
  209.3 10.5 %fusion.137 = f32[3,640]{1,0:T(4,128)S(1)} fusion(f32[3,640,2176]{2,1,0:T(8,128)} %get-tuple-element.568, f32[3,640]{1,0:T(4,128)S(1)} %get-tuple-element.569, pred[640,2176]{1,0:T(8,128)(4,1)S(1)} %fusion.135), kind=kLoop, calls=%fused_computation.8.clone.1 | loop fusion | flops 16709760 | bytes 18119680 | tf_op jit(solution)/shard_map/while/body/eval_jaxpr/reduce_sum | solution.py:171
  219.8 8.8 %fusion.138 = bf16[3,64,640]{2,1,0:T(8,128)(2,1)S(1)} fusion(bf16[2176,3,64]{0,2,1:T(8,128)(2,1)S(1)} %bitcast.144, f32[3,640,2176]{2,1,0:T(8,128)} %get-tuple-element.568, f32[3,640]{1,0:T(4,128)S(1)} %fusion.137, f32[3,640]{1,0:T(4,128)S(1)} %get-tuple-element.569, pred[640,2176]{1,0:T(8,128)(4,1)S(1)} %fusion.135), kind=kOutput, calls=%fused_computation.15.clone.1 | convolution fusion | flops 555786240 | bytes 19201024 | tf_op jit(solution)/shard_map/while/body/eval_jaxpr/hqk,khd->qhd/dot_general | solution.py:173
  231.1 4.8 fusion.135
  237.5 8.0 %fusion.136 = (f32[3,640]{1,0:T(4,128)S(1)}, f32[3,640,2176]{2,1,0:T(8,128)}) fusion(pred[640,2176]{1,0:T(8,128)(4,1)S(1)} %fusion.135, bf16[640,3,64]{0,2,1:T(8,128)(2,1)S(1)} %bitcast.146, bf16[2176,3,64]{0,2,1:T(8,128)(2,1)S(1)} %bitcast.145), kind=kOutput, calls=%fused_computation.7.clone.1 | convolution fusion | flops 547305600 | bytes 19193344 | tf_op jit(solution)/shard_map/while/body/eval_jaxpr/qhd,khd->hqk/dot_general | solution.py:162
  245.4 10.5 %fusion.137 = f32[3,640]{1,0:T(4,128)S(1)} fusion(f32[3,640,2176]{2,1,0:T(8,128)} %get-tuple-element.568, f32[3,640]{1,0:T(4,128)S(1)} %get-tuple-element.569, pred[640,2176]{1,0:T(8,128)(4,1)S(1)} %fusion.135), kind=kLoop, calls=%fused_computation.8.clone.1 | loop fusion | flops 16709760 | bytes 18119680 | tf_op jit(solution)/shard_map/while/body/eval_jaxpr/reduce_sum | solution.py:171
  255.9 8.8 %fusion.138 = bf16[3,64,640]{2,1,0:T(8,128)(2,1)S(1)} fusion(bf16[2176,3,64]{0,2,1:T(8,128)(2,1)S(1)} %bitcast.144, f32[3,640,2176]{2,1,0:T(8,128)} %get-tuple-element.568, f32[3,640]{1,0:T(4,128)S(1)} %fusion.137, f32[3,640]{1,0:T(4,128)S(1)} %get-tuple-element.569, pred[640,2176]{1,0:T(8,128)(4,1)S(1)} %fusion.135), kind=kOutput, calls=%fused_computation.15.clone.1 | convolution fusion | flops 555786240 | bytes 19201024 | tf_op jit(solution)/shard_map/while/body/eval_jaxpr/hqk,khd->qhd/dot_general | solution.py:173
  272.1 31.6 %reduce-scatter.5.cloned.1.call-done = bf16[320,768]{1,0:T(8,128)(2,1)} async-done(((bf16[1280,768]{1,0:T(8,128)(2,1)}), bf16[320,768]{1,0:T(8,128)(2,1)}) %reduce-scatter.5.cloned.1.call-update) | async-done | bytes 491536 | tf_op jit(solution)/shard_map/reduce_scatter | solution.py:181
  309.3 11.2 %collective-permute-done.2 = bf16[320,768]{1,0:T(8,128)(2,1)S(1)} collective-permute-done((bf16[320,768]{1,0:T(8,128)(2,1)S(1)}, bf16[320,768]{1,0:T(8,128)(2,1)S(1)}, u32[]{:S(2)}, u32[]{:S(2)}) %collective-permute-start.2) | collective-permute-done | bytes 491552 | tf_op jit(solution)/shard_map/ppermute | solution.py:19
  322.2 6.6 collective-permute-done.4
  329.6 5.5 fusion.64
  335.1 24.0 %all-gather.10.cloned.1.call-done = bf16[768,768]{0,1:T(8,128)(2,1)} async-done(((bf16[768,96]{0,1:T(8,128)(2,1)}), bf16[768,768]{0,1:T(8,128)(2,1)}) %all-gather.10.cloned.1.call-update) | async-done | bytes 1179664 | tf_op jit(solution)/shard_map/all_gather | solution.py:99
  359.1 21.6 %all-gather.12.cloned.1.call-done = bf16[1280,768]{1,0:T(8,128)(2,1)} async-done(((bf16[320,768]{1,0:T(8,128)(2,1)}), bf16[1280,768]{1,0:T(8,128)(2,1)}) %all-gather.12.cloned.1.call-update) | async-done | bytes 1966096 | tf_op jit(solution)/shard_map/all_gather | solution.py:200
  380.8 13.1 %add_convert_fusion = (bf16[1280,768]{1,0:T(8,128)(2,1)S(1)}, f32[1280,768]{1,0:T(8,128)}) fusion(f32[1280,768]{1,0:T(8,128)} %fusion.64, bf16[1280,768]{1,0:T(8,128)(2,1)} %all-gather.12.cloned.1.call-done, bf16[768,768]{0,1:T(8,128)(2,1)} %all-gather.10.cloned.1.call-done), kind=kOutput, calls=%fused_computation.47 | convolution fusion | flops 1580728320 | bytes 12976128 | tf_op jit(solution)/shard_map/td,fd->tf/dot_general | solution.py:202
  395.2 4.4 convolution_convert_fusion.1
  399.7 30.7 %reduce-scatter.9.cloned.1.call-done = bf16[320,768]{1,0:T(8,128)(2,1)} async-done(((bf16[1280,768]{1,0:T(8,128)(2,1)}), bf16[320,768]{1,0:T(8,128)(2,1)}) %reduce-scatter.9.cloned.1.call-update) | async-done | bytes 491536 | tf_op jit(solution)/shard_map/reduce_scatter | solution.py:210
  435.2 21.4 %all-gather.14.cloned.1.call-done = bf16[1280,768]{1,0:T(8,128)(2,1)} async-done(((bf16[320,768]{1,0:T(8,128)(2,1)}), bf16[1280,768]{1,0:T(8,128)(2,1)}) %all-gather.14.cloned.1.call-update) | async-done | bytes 1966096 | tf_op jit(solution)/shard_map/all_gather | solution.py:220
  462.9 112.5 %while.30 = (s32[]{:T(128)}, bf16[1280,192]{0,1:T(8,128)(2,1)}, f32[2816,384]{0,1:T(8,128)}, bf16[2816,384]{0,1:T(8,128)(2,1)}, s32[2816]{0:T(1024)S(1)}, /*inde...) while((s32[]{:T(128)}, bf16[1280,192]{0,1:T(8,128)(2,1)}, ...), condition=%wide.region_14.15_spmd.clone, body=%wide.region_12.14_spmd.clone.sunk | while | flops 2727729920 | bytes 220916592 | solution.py:269
  464.2 4.8 fusion.151
  470.6 8.1 %fusion.150 = f32[3,640,2176]{2,1,0:T(8,128)} fusion(bf16[640,3,64]{0,2,1:T(8,128)(2,1)S(1)} %bitcast.141, bf16[2176,3,64]{0,2,1:T(8,128)(2,1)S(1)} %bitcast.140), kind=kOutput, calls=%fused_computation.142.clone.1 | convolution fusion | flops 534773760 | bytes 17793024 | tf_op jit(solution)/shard_map/while/body/eval_jaxpr/qhd,khd->hqk/dot_general | solution.py:235
  478.7 15.1 %multiply_reduce_fusion.3 = (f32[3,640]{1,0:T(4,128)S(1)}, f32[3,640,2176]{2,1,0:T(8,128)}) fusion(f32[3,640,2176]{2,1,0:T(8,128)} %fusion.150, f32[3,640]{1,0:T(4,128)S(1)} %dynamic-slice_bitcast_fusion.2, bf16[640,3,64]{0,2,1:T(8,128)(2,1)S(1)} %bitcast.138, bf16[2176,3,64]{0,2,1:T(8,128)(2,1)S(1)} %bitcast.135, pred[640,2176]{1,0:T(8,128)(4,1)S(1)} %fusion.151), kind=kOutput, calls=%fused_computation.24.clone.1 | convolution fusion | flops 555661440 | bytes 35912704 | tf_op jit(solution)/shard_map/while/body/eval_jaxpr/qhd,khd->hqk/dot_general | solution.py:162
  493.8 11.4 %multiply_convert_fusion.5 = bf16[3,640,2176]{2,1,0:T(8,128)(2,1)S(1)} fusion(f32[3,640,2176]{2,1,0:T(8,128)} %get-tuple-element.585, f32[3,640,2176]{2,1,0:T(8,128)} %fusion.150, f32[3,640]{1,0:T(4,128)S(1)} %get-tuple-element.586), kind=kLoop, calls=%fused_computation.23.clone.1 | loop fusion | flops 12533760 | bytes 41786880 | tf_op jit(solution)/shard_map/while/body/eval_jaxpr/convert_element_type | solution.py:239
  505.2 3.9 copy-done
  514.8 4.4 fusion.153
  520.5 4.8 fusion.151
  526.8 8.1 %fusion.150 = f32[3,640,2176]{2,1,0:T(8,128)} fusion(bf16[640,3,64]{0,2,1:T(8,128)(2,1)S(1)} %bitcast.141, bf16[2176,3,64]{0,2,1:T(8,128)(2,1)S(1)} %bitcast.140), kind=kOutput, calls=%fused_computation.142.clone.1 | convolution fusion | flops 534773760 | bytes 17793024 | tf_op jit(solution)/shard_map/while/body/eval_jaxpr/qhd,khd->hqk/dot_general | solution.py:235
  534.9 15.1 %multiply_reduce_fusion.3 = (f32[3,640]{1,0:T(4,128)S(1)}, f32[3,640,2176]{2,1,0:T(8,128)}) fusion(f32[3,640,2176]{2,1,0:T(8,128)} %fusion.150, f32[3,640]{1,0:T(4,128)S(1)} %dynamic-slice_bitcast_fusion.2, bf16[640,3,64]{0,2,1:T(8,128)(2,1)S(1)} %bitcast.138, bf16[2176,3,64]{0,2,1:T(8,128)(2,1)S(1)} %bitcast.135, pred[640,2176]{1,0:T(8,128)(4,1)S(1)} %fusion.151), kind=kOutput, calls=%fused_computation.24.clone.1 | convolution fusion | flops 555661440 | bytes 35912704 | tf_op jit(solution)/shard_map/while/body/eval_jaxpr/qhd,khd->hqk/dot_general | solution.py:162
  550.1 11.4 %multiply_convert_fusion.5 = bf16[3,640,2176]{2,1,0:T(8,128)(2,1)S(1)} fusion(f32[3,640,2176]{2,1,0:T(8,128)} %get-tuple-element.585, f32[3,640,2176]{2,1,0:T(8,128)} %fusion.150, f32[3,640]{1,0:T(4,128)S(1)} %get-tuple-element.586), kind=kLoop, calls=%fused_computation.23.clone.1 | loop fusion | flops 12533760 | bytes 41786880 | tf_op jit(solution)/shard_map/while/body/eval_jaxpr/convert_element_type | solution.py:239
  561.5 3.9 copy-done
  571.1 4.3 fusion.153
  581.6 27.3 %collective-permute-done.6 = bf16[256,384]{0,1:T(8,128)(2,1)S(1)} collective-permute-done((bf16[256,384]{0,1:T(8,128)(2,1)S(1)}, bf16[256,384]{0,1:T(8,128)(2,1)S(1)}, u32[]{:S(2)}, u32[]{:S(2)}) %collective-permute-start.6) | collective-permute-done | bytes 196640 | tf_op jit(solution)/shard_map/ppermute | solution.py:32
  614.1 4.0 multiply_convert_fusion.1
  620.9 4.2 all-to-all-start.3
  625.2 4.3 convolution_convert_fusion.2
  642.3 11.3 %all-to-all-done.3 = bf16[8,768,96]{1,2,0:T(8,128)(2,1)} async-done(((bf16[8,768,96]{1,2,0:T(8,128)(2,1)}), bf16[8,768,96]{1,2,0:T(8,128)(2,1)}, u32[]{:S(2)}, u32[]{:S(2)}) %all-to-all-start.3) | async-done | bytes 1179680 | tf_op jit(solution)/shard_map/all_to_all | solution.py:43
  653.6 4.1 all-to-all-start.1
  661.7 6.4 all-reduce.4
  671.3 6.1 all-to-all-start
  677.4 4.9 convolution_convert_fusion.8
  685.8 15.5 %all-to-all-done = bf16[8,96,577]{2,1,0:T(8,128)(2,1)S(1)} async-done(((bf16[8,96,577]{2,1,0:T(8,128)(2,1)}), bf16[8,96,577]{2,1,0:T(8,128)(2,1)S(1)}, u32[]{:S(2)}, u32[]{:S(2)}) %all-to-all-start) | async-done | bytes 886304 | tf_op jit(solution)/shard_map/all_to_all | solution.py:43
  714.3 24.3 %all-to-all-done.2 = bf16[8,96,769]{2,1,0:T(8,128)(2,1)S(1)} async-done(((bf16[8,96,769]{2,1,0:T(8,128)(2,1)}), bf16[8,96,769]{2,1,0:T(8,128)(2,1)S(1)}, u32[]{:S(2)}, u32[]{:S(2)}) %all-to-all-start.2) | async-done | bytes 1181216 | tf_op jit(solution)/shard_map/all_to_all | solution.py:43
  (251 shorter events, 123.7 us)
Async XLA Ops:
  8.0 95.4 %all-gather.6.cloned.1.call-start = ((), (), s32[]{:S(2)}) async-start(), calls=%async_computation.8 | async-start | bytes 2457600 | tf_op jit(solution)/shard_map/all_gather | solution.py:117
  9.3 30.9 %copy-start.37 = (f32[320]{0:T(512)}, f32[320]{0:T(512)S(1)}, u32[]{:S(2)}) copy-start(f32[320]{0:T(512)S(1)} %add_rsqrt_fusion.1) | copy-start | bytes 3844
  39.2 264.4 %reduce-scatter.5.cloned.1.call-start = ((), (), s32[]{:S(2)}) async-start(), calls=%async_computation.9 | async-start | bytes 2457600 | tf_op jit(solution)/shard_map/reduce_scatter | solution.py:181
  72.2 36.3 %copy-start.19 = (bf16[768,192]{1,0:T(8,128)(2,1)}, bf16[768,192]{1,0:T(8,128)(2,1)S(1)}, u32[]{:S(2)}) copy-start(bf16[768,192]{1,0:T(8,128)(2,1)S(1)} %all_gather.35) | copy-start | bytes 884740
  103.4 52.9 %copy-start.21 = (bf16[768,192]{1,0:T(8,128)(2,1)}, bf16[768,192]{1,0:T(8,128)(2,1)S(1)}, u32[]{:S(2)}) copy-start(bf16[768,192]{1,0:T(8,128)(2,1)S(1)} %all_gather.36) | copy-start | bytes 884740
  103.4 52.9 %copy-start.36 = (bf16[96,192]{1,0:T(8,128)(2,1)S(1)}, bf16[96,192]{1,0:T(8,128)(2,1)}, u32[]{:S(2)}) copy-start(bf16[96,192]{1,0:T(8,128)(2,1)} %param.21) | copy-start | bytes 110596
  105.9 82.6 %copy-start.3 = (bf16[1280,768]{1,0:T(8,128)(2,1)S(1)}, bf16[1280,768]{1,0:T(8,128)(2,1)}, u32[]{:S(2)}) copy-start(bf16[1280,768]{1,0:T(8,128)(2,1)} %all-gather.6.cloned.1.call-done) | copy-start | bytes 5898244
  108.5 83.2 %collective-permute-start.1 = (bf16[1280,384]{0,1:T(8,128)(2,1)S(1)}, bf16[1280,384]{0,1:T(8,128)(2,1)S(1)}, u32[]{:S(2)}, u32[]{:S(2)}) collective-permute-start(bf16[1280,384]{0,1:T(8,128)(2,1)S(1)} %pad_maximum_fusion.1), channel_id=1, source_target_pairs={{0,4},{4,8},{8,12},{12,16},{16,20},{20,24},{24,28},{1,5},{5,9},{9,... | collective-permute-start | bytes 2949128 | tf_op jit(solution)/shard_map/ppermute | solution.py:32
  187.2 4.5 collective-permute-start
  219.8 8.9 %copy-start.27 = (bf16[2,640,192]{1,2,0:T(8,128)(2,1)S(1)}, bf16[2,640,192]{1,2,0:T(8,128)(2,1)}, u32[]{:S(2)}) copy-start(bf16[2,640,192]{1,2,0:T(8,128)(2,1)} %get-tuple-element.604) | copy-start | bytes 1474564 | tf_op jit(solution)/shard_map/while
  265.7 38.0 %copy-start.1 = (bf16[320,768]{1,0:T(8,128)(2,1)S(1)}, bf16[320,768]{1,0:T(8,128)(2,1)}, u32[]{:S(2)}) copy-start(bf16[320,768]{1,0:T(8,128)(2,1)} %param.16) | copy-start | bytes 1474564
  266.8 38.3 %copy-start.10 = (bf16[2,24,8,640]{3,2,0,1:T(8,128)(2,1)}, bf16[2,24,8,640]{3,2,0,1:T(8,128)(2,1)S(1)}, u32[]{:S(2)}) copy-start(bf16[2,24,8,640]{3,2,0,1:T(8,128)(2,1)S(1)} %copy.67) | copy-start | bytes 1474564
  270.0 59.6 %all-gather.8.cloned.1.call-start = ((), (), s32[]{:S(2)}) async-start(), calls=%async_computation.10 | async-start | bytes 1327104 | tf_op jit(solution)/shard_map/all_gather | solution.py:98
  270.6 88.5 %all-gather.10.cloned.1.call-start = ((), (), s32[]{:S(2)}) async-start(), calls=%async_computation.11 | async-start | bytes 1327104 | tf_op jit(solution)/shard_map/all_gather | solution.py:99
  271.2 109.6 %all-gather.12.cloned.1.call-start = ((), (), s32[]{:S(2)}) async-start(), calls=%async_computation.13 | async-start | bytes 2457600 | tf_op jit(solution)/shard_map/all_gather | solution.py:200
  271.8 158.6 %reduce-scatter.9.cloned.1.call-start = ((), (), s32[]{:S(2)}) async-start(), calls=%async_computation.14 | async-start | bytes 2457600 | tf_op jit(solution)/shard_map/reduce_scatter | solution.py:210
  272.0 160.5 %copy-start.30 = (f32[768]{0:T(1024)}, f32[768]{0:T(1024)S(1)}, u32[]{:S(2)}) copy-start(f32[768]{0:T(1024)S(1)} %convert_element_type.159) | copy-start | bytes 9220
  304.9 127.6 %copy-start.34 = (f32[320]{0:T(512)}, f32[320]{0:T(512)S(1)}, u32[]{:S(2)}) copy-start(f32[320]{0:T(512)S(1)} %add_rsqrt_fusion) | copy-start | bytes 3844
  307.6 12.9 %collective-permute-start.2 = (bf16[320,768]{1,0:T(8,128)(2,1)S(1)}, bf16[320,768]{1,0:T(8,128)(2,1)S(1)}, u32[]{:S(2)}, u32[]{:S(2)}) collective-permute-start(bf16[320,768]{1,0:T(8,128)(2,1)S(1)} %get-tuple-element.423), channel_id=1, source_target_pairs={{0,1},{1,2},{2,3},{3,0},{4,5},{5,6},{6,7},{7,4},{8,9},{9,10},{10,1... | collective-permute-start | bytes 1474568 | tf_op jit(solution)/shard_map/ppermute | solution.py:19
  307.6 13.8 %collective-permute-start.3 = (bf16[320,768]{1,0:T(8,128)(2,1)S(1)}, bf16[320,768]{1,0:T(8,128)(2,1)S(1)}, u32[]{:S(2)}, u32[]{:S(2)}) collective-permute-start(bf16[320,768]{1,0:T(8,128)(2,1)S(1)} %get-tuple-element.423), channel_id=1, source_target_pairs={{0,3},{1,0},{2,1},{3,2},{4,7},{5,4},{6,5},{7,6},{8,11},{9,8},{10,9... | collective-permute-start | bytes 1474568 | tf_op jit(solution)/shard_map/ppermute | solution.py:22
  320.5 8.3 %collective-permute-start.4 = (bf16[320,768]{1,0:T(8,128)(2,1)S(1)}, bf16[320,768]{1,0:T(8,128)(2,1)S(1)}, u32[]{:S(2)}, u32[]{:S(2)}) collective-permute-start(bf16[320,768]{1,0:T(8,128)(2,1)S(1)} %collective-permute-done.2), channel_id=1, source_target_pairs={{0,1},{1,2},{2,3},{3,0},{4,5},{5,6},{6,7},{7,4},{8,9},{9,10},{10,1... | collective-permute-start | bytes 1474568 | tf_op jit(solution)/shard_map/ppermute | solution.py:19
  395.2 35.2 %copy-start.5 = (bf16[320,768]{1,0:T(8,128)(2,1)S(1)}, bf16[320,768]{1,0:T(8,128)(2,1)}, u32[]{:S(2)}) copy-start(bf16[320,768]{1,0:T(8,128)(2,1)} %reduce-scatter.5.cloned.1.call-done) | copy-start | bytes 1474564
  395.2 37.4 %copy-start.7 = (bf16[320,768]{1,0:T(8,128)(2,1)S(1)}, bf16[320,768]{1,0:T(8,128)(2,1)}, u32[]{:S(2)}) copy-start(bf16[320,768]{1,0:T(8,128)(2,1)} %param.17) | copy-start | bytes 1474564
  399.6 57.0 %copy-start.25 = (bf16[192,768]{0,1:T(8,128)(2,1)S(1)}, bf16[192,768]{0,1:T(8,128)(2,1)}, u32[]{:S(2)}) copy-start(bf16[192,768]{0,1:T(8,128)(2,1)} %all_gather.38) | copy-start | bytes 884740
  399.6 57.0 %all-gather.14.cloned.1.call-start = ((), (), s32[]{:S(2)}) async-start(), calls=%async_computation.15 | async-start | bytes 2457600 | tf_op jit(solution)/shard_map/all_gather | solution.py:220
  432.6 30.4 %copy-start.39 = (f32[320]{0:T(512)}, f32[320]{0:T(512)S(1)}, u32[]{:S(2)}) copy-start(f32[320]{0:T(512)S(1)} %broadcast_multiply_fusion.1) | copy-start | bytes 3844
  434.8 225.4 %reduce-scatter.11.cloned.1.call-start = ((), (), s32[]{:S(2)}) async-start(), calls=%async_computation.16 | async-start | bytes 2457600 | tf_op jit(solution)/shard_map/reduce_scatter | solution.py:294
  493.8 15.3 %copy-start = (f32[3,640,2176]{2,1,0:T(8,128)S(1)}, f32[3,640,2176]{2,1,0:T(8,128)}, u32[]{:S(2)}) copy-start(f32[3,640,2176]{2,1,0:T(8,128)} %get-tuple-element.585) | copy-start | bytes 50135044 | tf_op jit(solution)/shard_map/while
  550.0 15.3 %copy-start = (f32[3,640,2176]{2,1,0:T(8,128)S(1)}, f32[3,640,2176]{2,1,0:T(8,128)}, u32[]{:S(2)}) copy-start(f32[3,640,2176]{2,1,0:T(8,128)} %get-tuple-element.585) | copy-start | bytes 50135044 | tf_op jit(solution)/shard_map/while
  578.0 30.9 %collective-permute-start.5 = (bf16[1280,384]{0,1:T(8,128)(2,1)S(1)}, bf16[1280,384]{0,1:T(8,128)(2,1)S(1)}, u32[]{:S(2)}, u32[]{:S(2)}) collective-permute-start(bf16[1280,384]{0,1:T(8,128)(2,1)S(1)} %slice.58), channel_id=1, source_target_pairs={{4,0},{8,4},{12,8},{16,12},{20,16},{24,20},{28,24},{5,1},{9,5},{13... | collective-permute-start | bytes 2949128 | tf_op jit(solution)/shard_map/ppermute | solution.py:32
  579.5 29.4 %collective-permute-start.6 = (bf16[256,384]{0,1:T(8,128)(2,1)S(1)}, bf16[256,384]{0,1:T(8,128)(2,1)S(1)}, u32[]{:S(2)}, u32[]{:S(2)}) collective-permute-start(bf16[256,384]{0,1:T(8,128)(2,1)S(1)} %slice.59), channel_id=1, source_target_pairs={{8,0},{12,4},{16,8},{20,12},{24,16},{28,20},{9,1},{13,5},{17,9},{2... | collective-permute-start | bytes 589832 | tf_op jit(solution)/shard_map/ppermute | solution.py:32
  580.8 29.9 %copy-start.20 = (bf16[768,192]{1,0:T(8,128)(2,1)S(1)}, bf16[768,192]{1,0:T(8,128)(2,1)}, u32[]{:S(2)}) copy-start(bf16[768,192]{1,0:T(8,128)(2,1)} %copy-done.19) | copy-start | bytes 884740
  620.9 32.7 %all-to-all-start.3 = ((bf16[8,768,96]{1,2,0:T(8,128)(2,1)}), bf16[8,768,96]{1,2,0:T(8,128)(2,1)}, u32[]{:S(2)}, u32[]{:S(2)}) async-start(bf16[8,768,96]{1,2,0:T(8,128)(2,1)} %bitcast.154), calls=%async_computation.7 | async-start | bytes 2359296 | tf_op jit(solution)/shard_map/all_to_all | solution.py:43
  625.2 84.5 %reduce-scatter.7.cloned.1.call-start = ((), (), s32[]{:S(2)}) async-start(), calls=%async_computation.12 | async-start | bytes 2457600 | tf_op jit(solution)/shard_map/reduce_scatter | solution.py:193
  633.9 23.9 %copy-start.18 = (bf16[1280,384]{0,1:T(8,128)(2,1)S(1)}, bf16[1280,384]{0,1:T(8,128)(2,1)}, u32[]{:S(2)}) copy-start(bf16[1280,384]{0,1:T(8,128)(2,1)} %copy-done.17) | copy-start | bytes 2949124
  638.1 22.1 %copy-start.2 = (bf16[320,768]{1,0:T(8,128)(2,1)S(1)}, bf16[320,768]{1,0:T(8,128)(2,1)}, u32[]{:S(2)}) copy-start(bf16[320,768]{1,0:T(8,128)(2,1)} %param.16) | copy-start | bytes 1474564
  638.1 22.1 %copy-start.33 = (f32[768]{0:T(1024)S(1)}, f32[768]{0:T(1024)}, u32[]{:S(2)}) copy-start(f32[768]{0:T(1024)} %copy-done.32) | copy-start | bytes 9220
  638.1 22.1 %copy-start.38 = (f32[320]{0:T(512)S(1)}, f32[320]{0:T(512)}, u32[]{:S(2)}) copy-start(f32[320]{0:T(512)} %copy-done.37) | copy-start | bytes 3844
  638.1 23.7 %copy-start.41 = (f32[768]{0:T(1024)S(1)}, f32[768]{0:T(1024)}, u32[]{:S(2)}) copy-start(f32[768]{0:T(1024)} %get-tuple-element.370) | copy-start | bytes 9220
  653.6 17.6 %all-to-all-start.1 = ((bf16[8,192,96]{2,1,0:T(8,128)(2,1)}), bf16[8,192,96]{2,1,0:T(8,128)(2,1)}, u32[]{:S(2)}, u32[]{:S(2)}) async-start(bf16[8,192,96]{2,1,0:T(8,128)(2,1)} %bitcast.150), calls=%async_computation.5 | async-start | bytes 786432 | tf_op jit(solution)/shard_map/all_to_all | solution.py:43
  671.3 30.0 %all-to-all-start = ((bf16[8,96,577]{2,1,0:T(8,128)(2,1)}), bf16[8,96,577]{2,1,0:T(8,128)(2,1)S(1)}, u32[]{:S(2)}, u32[]{:S(2)}) async-start(bf16[8,96,577]{2,1,0:T(8,128)(2,1)} %pad_maximum_fusion.2), calls=%async_computation.4 | async-start | bytes 1966080 | tf_op jit(solution)/shard_map/all_to_all | solution.py:43
  682.3 27.4 %copy-start.6 = (bf16[320,768]{1,0:T(8,128)(2,1)S(1)}, bf16[320,768]{1,0:T(8,128)(2,1)}, u32[]{:S(2)}) copy-start(bf16[320,768]{1,0:T(8,128)(2,1)} %reduce-scatter.5.cloned.1.call-done) | copy-start | bytes 1474564
  682.3 27.4 %copy-start.8 = (bf16[320,768]{1,0:T(8,128)(2,1)S(1)}, bf16[320,768]{1,0:T(8,128)(2,1)}, u32[]{:S(2)}) copy-start(bf16[320,768]{1,0:T(8,128)(2,1)} %param.17) | copy-start | bytes 1474564
  682.3 27.4 %copy-start.9 = (bf16[320,768]{1,0:T(8,128)(2,1)S(1)}, bf16[320,768]{1,0:T(8,128)(2,1)}, u32[]{:S(2)}) copy-start(bf16[320,768]{1,0:T(8,128)(2,1)} %reduce-scatter.9.cloned.1.call-done) | copy-start | bytes 1474564
  682.3 27.4 %copy-start.31 = (f32[768]{0:T(1024)S(1)}, f32[768]{0:T(1024)}, u32[]{:S(2)}) copy-start(f32[768]{0:T(1024)} %copy-done.30) | copy-start | bytes 9220
  682.3 27.4 %copy-start.35 = (f32[320]{0:T(512)S(1)}, f32[320]{0:T(512)}, u32[]{:S(2)}) copy-start(f32[320]{0:T(512)} %copy-done.34) | copy-start | bytes 3844
  682.3 27.4 %copy-start.40 = (f32[320]{0:T(512)S(1)}, f32[320]{0:T(512)}, u32[]{:S(2)}) copy-start(f32[320]{0:T(512)} %copy-done.39) | copy-start | bytes 3844
  702.2 36.4 %all-to-all-start.2 = ((bf16[8,96,769]{2,1,0:T(8,128)(2,1)}), bf16[8,96,769]{2,1,0:T(8,128)(2,1)S(1)}, u32[]{:S(2)}, u32[]{:S(2)}) async-start(bf16[8,96,769]{2,1,0:T(8,128)(2,1)} %pad_maximum_fusion), calls=%async_computation.6 | async-start | bytes 2752512 | tf_op jit(solution)/shard_map/all_to_all | solution.py:43
  (23 other events, 79.2 us)
Sparse Core Ops, SparseCore 0:
  39.3 19.0 all-gather.5
  270.1 33.4 reduce-scatter.4
  399.7 30.6 reduce-scatter.8
Sparse Core Ops, SparseCore 1:
  272.7 44.3 all-gather.7
  319.1 40.0 all-gather.9
  360.6 20.1 all-gather.11
  434.9 21.7 all-gather.13
  614.2 28.7 reduce-scatter.10
  645.7 30.8 reduce-scatter.6
